TPU v7x, 256 devices: a whole 4x4x8 slice. The times are simulated.
256 devices in a mesh: ctx: 64 (over y, z, core), ch: 4 (over x).
Axes of the slice: x: 4, y: 4, z: 8, core: 2. Of those that a mesh axis runs over, the one named last changes fastest.
Arguments:
- q_in: bfloat16 [8192, 4096], P('ctx', 'ch'), may hold values from -6 to 6
- k_in: bfloat16 [8192, 4096], P('ctx', 'ch'), may hold values from -6 to 6
- v_in: bfloat16 [8192, 4096], P('ctx', 'ch'), may hold values from -6 to 6
- short_taps: float32 [3, 3, 4096], P(None, None, 'ch'), may hold values from -3 to 3
- skip_bias: float32 [4096], P('ch'), may hold values from -4.5 to 4.5
- norm_gain: float32 [4096], P('ch'), may hold values from 0.1 to 1.9
- filter_spectrum: float32 [2, 64, 2, 128, 4096], P(None, 'ctx', None, None, 'ch'), may hold values from -6 to 6
Outputs:
- mixer_out: bfloat16 [8192, 4096], P('ctx', 'ch')
All inputs are finite; a program needn't handle non-finite values.
Results may differ from a plain program's by a relative error of at most 0.001.
Values may be sent and summed in bfloat16 or wider, within the bound.
A program may use at most 64 MiB of HBM per device.

v0:
```python
import math

import jax
import jax.numpy as jnp
from jax import lax
from jax.sharding import PartitionSpec as P

norm_eps = 1e-06
full_turn = 2.0 * math.pi


def from_behind(block, axis, distance):
    devices = range(lax.axis_size(axis))
    route = [(i - distance, i) for i in devices if i - distance in devices]
    return lax.ppermute(block, axis, route)


def partner_2(value, axis, bit):
    return lax.ppermute(value, axis, [(i, i ^ 1 << bit) for i in range(lax.axis_size(axis))])


def bit_reverse(positions, levels):
    result = jnp.zeros_like(positions)
    for bit_pos in range(levels):
        result = result + (positions >> bit_pos & 1) * (1 << levels - 1 - bit_pos)
    return result


def phase_of(numer, modulus):
    return full_turn * (numer % modulus).astype(jnp.float32) / modulus


def rotate(real_part, imag_part, phase):
    cosine = jnp.cos(phase)
    sine = jnp.sin(phase)
    return (real_part * cosine - imag_part * sine, real_part * sine + imag_part * cosine)


def product(table, operand, form):
    return jnp.einsum(form, table, operand, precision=lax.Precision.HIGHEST)


def per_device(q_in, k_in, v_in, short_taps, skip_bias, norm_gain, filter_spectrum):
    tok_rows, chan_cols = q_in.shape
    tap_count = short_taps.shape[1]
    devices = lax.axis_size("ctx")
    levels = devices.bit_length() - 1
    position = lax.axis_index("ctx")
    blocks = 2 * devices
    full_len = blocks * tok_rows
    stacked = jnp.stack((q_in, k_in, v_in))
    earlier = from_behind(stacked[:, tok_rows - tap_count + 1 :], "ctx", 1)
    extended = jnp.concatenate((earlier, stacked), axis=1).astype(jnp.float32)
    mixes = jnp.zeros(stacked.shape, jnp.float32)
    for lag_step in range(tap_count):
        begin = tap_count - 1 - lag_step
        mixes = mixes + short_taps[:, lag_step][:, None, :] * extended[:, begin : begin + tok_rows]
    query = mixes[0]
    mixed = mixes[1] * mixes[2]
    row_ids = jnp.arange(tok_rows, dtype=jnp.int32)
    local_phase = phase_of(row_ids[:, None] * row_ids[None, :], tok_rows)
    cos_local = jnp.cos(local_phase)
    sin_local = jnp.sin(local_phase)
    rev_index = bit_reverse(position, levels)
    odd_real, odd_imag = rotate(mixed, jnp.zeros_like(mixed), -phase_of(position, blocks))
    state = jnp.stack((jnp.stack((mixed, odd_real)), jnp.stack((jnp.zeros_like(mixed), odd_imag))))
    for bit_pos in range(levels - 1, -1, -1):
        stride = 1 << bit_pos
        partner = partner_2(state, "ctx", bit_pos)
        upper_side = position >> bit_pos & 1 == 1
        diff_real, diff_imag = rotate(
            partner[0] - state[0],
            partner[1] - state[1],
            -phase_of(position & stride - 1, 2 * stride),
        )
        state = jnp.where(upper_side, jnp.stack((diff_real, diff_imag)), state + partner)
    freq_rows = 2 * rev_index + jnp.arange(2, dtype=jnp.int32)
    twist = phase_of(row_ids[None, :] * freq_rows[:, None], full_len)[:, :, None]
    turned_real, turned_imag = rotate(state[0], state[1], -twist)
    spec_real = product(cos_local, turned_real, "sj,tjc->tsc") + product(
        sin_local, turned_imag, "sj,tjc->tsc"
    )
    spec_imag = product(cos_local, turned_imag, "sj,tjc->tsc") - product(
        sin_local, turned_real, "sj,tjc->tsc"
    )
    filt_real = filter_spectrum[0, 0]
    filt_imag = filter_spectrum[1, 0]
    prod_real = spec_real * filt_real - spec_imag * filt_imag
    prod_imag = spec_real * filt_imag + spec_imag * filt_real
    back_real = product(cos_local, prod_real, "js,tsc->tjc") - product(
        sin_local, prod_imag, "js,tsc->tjc"
    )
    back_imag = product(cos_local, prod_imag, "js,tsc->tjc") + product(
        sin_local, prod_real, "js,tsc->tjc"
    )
    back_real, back_imag = rotate(back_real, back_imag, twist)
    state = jnp.stack((back_real, back_imag))
    for bit_pos in range(levels):
        stride = 1 << bit_pos
        partner = partner_2(state, "ctx", bit_pos)
        upper_side = position >> bit_pos & 1 == 1
        phase = phase_of(position & stride - 1, 2 * stride)
        self_real, self_imag = rotate(state[0], state[1], phase)
        part_real, part_imag = rotate(partner[0], partner[1], phase)
        lower_value = jnp.stack((state[0] + part_real, state[1] + part_imag))
        upper_value = jnp.stack((partner[0] - self_real, partner[1] - self_imag))
        state = jnp.where(upper_side, upper_value, lower_value)
    edge = phase_of(position, blocks)
    conv_out = (state[0, 0] + jnp.cos(edge) * state[0, 1] - jnp.sin(edge) * state[1, 1]) / full_len
    gated = query * (conv_out + skip_bias * mixed)
    row_squares = lax.psum(jnp.sum(gated * gated, axis=1), "ch")
    mean_square = row_squares / (chan_cols * lax.axis_size("ch"))
    return (gated * lax.rsqrt(mean_square + norm_eps)[:, None] * norm_gain).astype(jnp.bfloat16)


def solution(mesh):
    placed = (
        P("ctx", "ch"),
        P("ctx", "ch"),
        P("ctx", "ch"),
        P(None, None, "ch"),
        P("ch"),
        P("ch"),
        P(None, "ctx", None, None, "ch"),
    )
    return jax.shard_map(
        per_device, mesh=mesh, in_specs=placed, out_specs=P("ctx", "ch"), check_vma=False
    )
```

profile of v0, /device:TPU:1, one launch (start us, length us, event | category | flops | bytes accessed | tf_op | source)
XLA Modules:
  0.0 746.5 jit_solution(17904887007825188924)
XLA Ops:
  4.0 4.9 collective-permute-start
  10.8 2.4 fusion
  18.1 2.9 collective-permute-start.1
  21.2 41.9 %collective-permute-done.1 = f32[2,2,128,1024]{2,3,1,0:T(8,128)S(1)} collective-permute-done((f32[2,2,128,1024]{2,3,1,0:T(8,128)}, f32[2,2,128,1024]{2,3,1,0:T(8,128)S(1)}, u32[]{:S(2)}, u32[]{:S(2)}) %collective-permute-start.1) | collective-permute-done | bytes 2097184 | tf_op jit(solution)/shard_map/ppermute | solution.py:19
  67.9 41.5 %collective-permute-done.2 = f32[2,2,128,1024]{2,3,1,0:T(8,128)} collective-permute-done((f32[2,2,128,1024]{2,3,1,0:T(8,128)}, f32[2,2,128,1024]{2,3,1,0:T(8,128)}, u32[]{:S(2)}, u32[]{:S(2)}) %collective-permute-start.2) | collective-permute-done | bytes 2097184 | tf_op jit(solution)/shard_map/ppermute | solution.py:19
  109.4 2.5 multiply_subtract_fusion.6
  111.9 3.6 maximum_select_fusion.1
  115.5 8.0 %collective-permute-start.3 = (f32[2,2,128,1024]{2,3,1,0:T(8,128)}, f32[2,2,128,1024]{2,3,1,0:T(8,128)S(1)}, u32[]{:S(2)}, u32[]{:S(2)}) collective-permute-start(f32[2,2,128,1024]{2,3,1,0:T(8,128)} %maximum_select_fusion.1), channel_id=1, source_target_pairs={{0,32},{4,36},{8,40},{12,44},{16,48},{20,52},{24,56},{28,60},{32,0... | collective-permute-start | bytes 6291464 | tf_op jit(solution)/shard_map/ppermute | solution.py:19
  123.7 41.9 %collective-permute-done.3 = f32[2,2,128,1024]{2,3,1,0:T(8,128)S(1)} collective-permute-done((f32[2,2,128,1024]{2,3,1,0:T(8,128)}, f32[2,2,128,1024]{2,3,1,0:T(8,128)S(1)}, u32[]{:S(2)}, u32[]{:S(2)}) %collective-permute-start.3) | collective-permute-done | bytes 2097184 | tf_op jit(solution)/shard_map/ppermute | solution.py:19
  165.6 2.6 multiply_subtract_fusion.5
  168.2 2.5 maximum_select_fusion.2
  170.8 51.3 %collective-permute-start.4 = (f32[2,2,128,1024]{2,3,1,0:T(8,128)S(1)}, f32[2,2,128,1024]{2,3,1,0:T(8,128)}, u32[]{:S(2)}, u32[]{:S(2)}) collective-permute-start(f32[2,2,128,1024]{2,3,1,0:T(8,128)S(1)} %maximum_select_fusion.2), channel_id=1, source_target_pairs={{0,16},{4,20},{8,24},{12,28},{16,0},{20,4},{24,8},{28,12},{32,48},... | collective-permute-start | bytes 6291464 | tf_op jit(solution)/shard_map/ppermute | solution.py:19
  222.2 90.2 %collective-permute-done.4 = f32[2,2,128,1024]{2,3,1,0:T(8,128)} collective-permute-done((f32[2,2,128,1024]{2,3,1,0:T(8,128)S(1)}, f32[2,2,128,1024]{2,3,1,0:T(8,128)}, u32[]{:S(2)}, u32[]{:S(2)}) %collective-permute-start.4) | collective-permute-done | bytes 2097184 | tf_op jit(solution)/shard_map/ppermute | solution.py:19
  314.3 3.2 maximum_select_fusion.3
  318.8 44.9 %collective-permute-done.5 = f32[2,2,128,1024]{2,3,1,0:T(8,128)S(1)} collective-permute-done((f32[2,2,128,1024]{2,3,1,0:T(8,128)}, f32[2,2,128,1024]{2,3,1,0:T(8,128)S(1)}, u32[]{:S(2)}, u32[]{:S(2)}) %collective-permute-start.5) | collective-permute-done | bytes 2097184 | tf_op jit(solution)/shard_map/ppermute | solution.py:19
  363.6 2.6 multiply_subtract_fusion.3
  366.2 2.5 maximum_select_fusion.4
  368.8 2.4 collective-permute-start.6
  371.2 3.1 fusion.87
  375.8 2.5 copy.32
  393.0 4.1 collective-permute-done.7
  399.1 46.0 %collective-permute-done.8 = f32[2,2,128,1024]{2,3,1,0:T(8,128)} collective-permute-done((f32[2,2,128,1024]{2,3,1,0:T(8,128)S(1)}, f32[2,2,128,1024]{2,3,1,0:T(8,128)}, u32[]{:S(2)}, u32[]{:S(2)}) %collective-permute-start.8) | collective-permute-done | bytes 2097184 | tf_op jit(solution)/shard_map/ppermute | solution.py:19
  445.1 2.1 subtract_add_fusion.4
  447.4 2.9 collective-permute-start.9
  450.5 89.9 %collective-permute-done.9 = f32[2,2,128,1024]{2,3,1,0:T(8,128)} collective-permute-done((f32[2,2,128,1024]{2,3,1,0:T(8,128)S(1)}, f32[2,2,128,1024]{2,3,1,0:T(8,128)}, u32[]{:S(2)}, u32[]{:S(2)}) %collective-permute-start.9) | collective-permute-done | bytes 2097184 | tf_op jit(solution)/shard_map/ppermute | solution.py:19
  540.4 2.1 subtract_add_fusion.3
  542.7 5.3 collective-permute-start.10
  548.1 89.6 %collective-permute-done.10 = f32[2,2,128,1024]{2,3,1,0:T(8,128)} collective-permute-done((f32[2,2,128,1024]{2,3,1,0:T(8,128)S(1)}, f32[2,2,128,1024]{2,3,1,0:T(8,128)}, u32[]{:S(2)}, u32[]{:S(2)}) %collective-permute-start.10) | collective-permute-done | bytes 2097184 | tf_op jit(solution)/shard_map/ppermute | solution.py:19
  641.6 43.3 %collective-permute-done.11 = f32[2,2,128,1024]{2,3,1,0:T(8,128)} collective-permute-done((f32[2,2,128,1024]{2,3,1,0:T(8,128)S(1)}, f32[2,2,128,1024]{2,3,1,0:T(8,128)}, u32[]{:S(2)}, u32[]{:S(2)}) %collective-permute-start.11) | collective-permute-done | bytes 2097184 | tf_op jit(solution)/shard_map/ppermute | solution.py:19
  687.2 3.0 collective-permute-start.12
  690.5 42.1 %collective-permute-done.12 = f32[2,2,128,1024]{2,3,1,0:T(8,128)} collective-permute-done((f32[2,2,128,1024]{2,3,1,0:T(8,128)S(1)}, f32[2,2,128,1024]{2,3,1,0:T(8,128)}, u32[]{:S(2)}, u32[]{:S(2)}) %collective-permute-start.12) | collective-permute-done | bytes 2097184 | tf_op jit(solution)/shard_map/ppermute | solution.py:19
  737.0 8.4 %psum.7 = f32[128]{0:T(128)S(1)} all-reduce(f32[128]{0:T(128)S(1)} %get-tuple-element.5), channel_id=1, replica_groups=mesh['ctx'=64,'ch'=4] {'ch'}, use_global_device_ids=true, to_apply=%region_1.2 | all-reduce | flops 128 | bytes 1024 | tf_op jit(solution)/shard_map/psum | solution.py:111
  (89 shorter events, 47.8 us)
Async XLA Ops:
  0.0 8.9 %copy-start.15 = (f32[3,3,1024]{2,1,0:T(4,128)S(1)}, f32[3,3,1024]{2,1,0:T(4,128)}, u32[]{:S(2)}) copy-start(f32[3,3,1024]{2,1,0:T(4,128)} %param.10) | copy-start | bytes 110596
  4.0 5.8 collective-permute-start
  13.1 1.2 copy-start.11
  13.2 1.3 copy-start.3
  13.2 1.5 copy-start.13
  14.7 0.8 copy-start.12
  15.6 1.0 copy-start
  18.1 45.0 %collective-permute-start.1 = (f32[2,2,128,1024]{2,3,1,0:T(8,128)}, f32[2,2,128,1024]{2,3,1,0:T(8,128)S(1)}, u32[]{:S(2)}, u32[]{:S(2)}) collective-permute-start(f32[2,2,128,1024]{2,3,1,0:T(8,128)} %pad_maximum_fusion), channel_id=1, source_target_pairs={{0,128},{4,132},{8,136},{12,140},{16,144},{20,148},{24,152},{28,15... | collective-permute-start | bytes 6291464 | tf_op jit(solution)/shard_map/ppermute | solution.py:19
  21.2 43.5 %copy-start.1 = (f32[1,2,128,1024]{2,3,1,0:T(8,128)S(1)}, f32[1,2,128,1024]{2,3,1,0:T(8,128)}, u32[]{:S(2)}) copy-start(f32[1,2,128,1024]{2,3,1,0:T(8,128)} %copy-done) | copy-start | bytes 3145732
  64.7 1.9 copy-start.5
  64.7 2.1 copy-start.7
  66.8 42.6 %collective-permute-start.2 = (f32[2,2,128,1024]{2,3,1,0:T(8,128)}, f32[2,2,128,1024]{2,3,1,0:T(8,128)}, u32[]{:S(2)}, u32[]{:S(2)}) collective-permute-start(f32[2,2,128,1024]{2,3,1,0:T(8,128)} %maximum_select_fusion), channel_id=1, source_target_pairs={{0,64},{4,68},{8,72},{12,76},{16,80},{20,84},{24,88},{28,92},{32,9... | collective-permute-start | bytes 6291464 | tf_op jit(solution)/shard_map/ppermute | solution.py:19
  67.9 44.0 %copy-start.2 = (f32[1,2,128,1024]{2,3,1,0:T(8,128)S(1)}, f32[1,2,128,1024]{2,3,1,0:T(8,128)}, u32[]{:S(2)}) copy-start(f32[1,2,128,1024]{2,3,1,0:T(8,128)} %copy-done) | copy-start | bytes 3145732
  67.9 44.0 %copy-start.6 = (f32[1,2,128,1024]{2,3,1,0:T(8,128)S(1)}, f32[1,2,128,1024]{2,3,1,0:T(8,128)}, u32[]{:S(2)}) copy-start(f32[1,2,128,1024]{2,3,1,0:T(8,128)} %copy-done.5) | copy-start | bytes 3145732
  67.9 44.0 %copy-start.8 = (f32[1,2,128,1024]{2,3,1,0:T(8,128)S(1)}, f32[1,2,128,1024]{2,3,1,0:T(8,128)}, u32[]{:S(2)}) copy-start(f32[1,2,128,1024]{2,3,1,0:T(8,128)} %copy-done.7) | copy-start | bytes 3145732
  115.5 50.1 %collective-permute-start.3 = (f32[2,2,128,1024]{2,3,1,0:T(8,128)}, f32[2,2,128,1024]{2,3,1,0:T(8,128)S(1)}, u32[]{:S(2)}, u32[]{:S(2)}) collective-permute-start(f32[2,2,128,1024]{2,3,1,0:T(8,128)} %maximum_select_fusion.1), channel_id=1, source_target_pairs={{0,32},{4,36},{8,40},{12,44},{16,48},{20,52},{24,56},{28,60},{32,0... | collective-permute-start | bytes 6291464 | tf_op jit(solution)/shard_map/ppermute | solution.py:19
  165.6 2.6 copy-start.9
  170.8 141.7 %collective-permute-start.4 = (f32[2,2,128,1024]{2,3,1,0:T(8,128)S(1)}, f32[2,2,128,1024]{2,3,1,0:T(8,128)}, u32[]{:S(2)}, u32[]{:S(2)}) collective-permute-start(f32[2,2,128,1024]{2,3,1,0:T(8,128)S(1)} %maximum_select_fusion.2), channel_id=1, source_target_pairs={{0,16},{4,20},{8,24},{12,28},{16,0},{20,4},{24,8},{28,12},{32,48},... | collective-permute-start | bytes 6291464 | tf_op jit(solution)/shard_map/ppermute | solution.py:19
  317.5 46.1 %collective-permute-start.5 = (f32[2,2,128,1024]{2,3,1,0:T(8,128)}, f32[2,2,128,1024]{2,3,1,0:T(8,128)S(1)}, u32[]{:S(2)}, u32[]{:S(2)}) collective-permute-start(f32[2,2,128,1024]{2,3,1,0:T(8,128)} %maximum_select_fusion.3), channel_id=1, source_target_pairs={{0,8},{4,12},{8,0},{12,4},{16,24},{20,28},{24,16},{28,20},{32,40},... | collective-permute-start | bytes 6291464 | tf_op jit(solution)/shard_map/ppermute | solution.py:19
  363.6 2.6 copy-start.10
  368.8 9.8 %collective-permute-start.6 = (f32[2,2,128,1024]{2,3,1,0:T(8,128)S(1)}, f32[2,2,128,1024]{2,3,1,0:T(8,128)}, u32[]{:S(2)}, u32[]{:S(2)}) collective-permute-start(f32[2,2,128,1024]{2,3,1,0:T(8,128)S(1)} %maximum_select_fusion.4), channel_id=1, source_target_pairs={{0,4},{4,0},{8,12},{12,8},{16,20},{20,16},{24,28},{28,24},{32,36},... | collective-permute-start | bytes 6291464 | tf_op jit(solution)/shard_map/ppermute | solution.py:19
  384.7 1.3 copy-start.14
  392.7 4.5 collective-permute-start.7
  397.8 47.3 %collective-permute-start.8 = (f32[2,2,128,1024]{2,3,1,0:T(8,128)S(1)}, f32[2,2,128,1024]{2,3,1,0:T(8,128)}, u32[]{:S(2)}, u32[]{:S(2)}) collective-permute-start(f32[2,2,128,1024]{2,3,1,0:T(8,128)S(1)} %maximum_select_fusion.6), channel_id=1, source_target_pairs={{0,8},{4,12},{8,0},{12,4},{16,24},{20,28},{24,16},{28,20},{32,40},... | collective-permute-start | bytes 6291464 | tf_op jit(solution)/shard_map/ppermute | solution.py:19
  447.4 93.0 %collective-permute-start.9 = (f32[2,2,128,1024]{2,3,1,0:T(8,128)S(1)}, f32[2,2,128,1024]{2,3,1,0:T(8,128)}, u32[]{:S(2)}, u32[]{:S(2)}) collective-permute-start(f32[2,2,128,1024]{2,3,1,0:T(8,128)S(1)} %maximum_select_fusion.7), channel_id=1, source_target_pairs={{0,16},{4,20},{8,24},{12,28},{16,0},{20,4},{24,8},{28,12},{32,48},... | collective-permute-start | bytes 6291464 | tf_op jit(solution)/shard_map/ppermute | solution.py:19
  542.7 95.1 %collective-permute-start.10 = (f32[2,2,128,1024]{2,3,1,0:T(8,128)S(1)}, f32[2,2,128,1024]{2,3,1,0:T(8,128)}, u32[]{:S(2)}, u32[]{:S(2)}) collective-permute-start(f32[2,2,128,1024]{2,3,1,0:T(8,128)S(1)} %maximum_select_fusion.8), channel_id=1, source_target_pairs={{0,32},{4,36},{8,40},{12,44},{16,48},{20,52},{24,56},{28,60},{32,0... | collective-permute-start | bytes 6291464 | tf_op jit(solution)/shard_map/ppermute | solution.py:19
  640.1 44.8 %collective-permute-start.11 = (f32[2,2,128,1024]{2,3,1,0:T(8,128)S(1)}, f32[2,2,128,1024]{2,3,1,0:T(8,128)}, u32[]{:S(2)}, u32[]{:S(2)}) collective-permute-start(f32[2,2,128,1024]{2,3,1,0:T(8,128)S(1)} %maximum_select_fusion.9), channel_id=1, source_target_pairs={{0,64},{4,68},{8,72},{12,76},{16,80},{20,84},{24,88},{28,92},{32,9... | collective-permute-start | bytes 6291464 | tf_op jit(solution)/shard_map/ppermute | solution.py:19
  687.2 45.4 %collective-permute-start.12 = (f32[2,2,128,1024]{2,3,1,0:T(8,128)S(1)}, f32[2,2,128,1024]{2,3,1,0:T(8,128)}, u32[]{:S(2)}, u32[]{:S(2)}) collective-permute-start(f32[2,2,128,1024]{2,3,1,0:T(8,128)S(1)} %maximum_select_fusion.10), channel_id=1, source_target_pairs={{0,128},{4,132},{8,136},{12,140},{16,144},{20,148},{24,152},{28,15... | collective-permute-start | bytes 6291464 | tf_op jit(solution)/shard_map/ppermute | solution.py:19
  734.7 1.0 copy-start.4
  734.7 1.0 copy-start.16
  735.7 9.7 %copy-start.17 = (f32[1024]{0:T(1024)S(1)}, f32[1024]{0:T(1024)}, u32[]{:S(2)}) copy-start(f32[1024]{0:T(1024)} %param.12) | copy-start | bytes 12292
where the time goes:
time: 754 us; the launch traced here: 747 us
  waiting for transfers between devices  576 us (76%)
  starting transfers between devices  85.6 us (11%)
  other arithmetic  47.4 us (6%)
  local copies, waits for them, and re-layouts  16.4 us (2%)
  matrix products  10.3 us (1%)
  blocking collectives  8.41 us (1%)
    ppermute x12, waiting for transfers between devices, partner_2(): lax.ppermute(value, axis, [(i, i ^ 1 << bit) for i in range(lax.axis_size...  575 us
    ppermute x12, starting transfers between devices, partner_2(): lax.ppermute(value, axis, [(i, i ^ 1 << bit) for i in range(lax.axis_size...  80.7 us
    select_n x6, other arithmetic, per_device(): jnp.where(upper_side, jnp.stack((diff_real, diff_imag)), state + partner)  15.7 us
  transfers between devices with their start and end apart: 13, of which 12 were waited for; matrix products, arithmetic and copies ran while one was open for 1% of the time, Pallas kernels for 0%

commit v1 on v0

v1 whole, which is shorter than its diff:
```python
import functools

import jax
import jax.numpy as jnp
import numpy as np
from jax import lax
from jax.experimental import pallas as pl
from jax.experimental.pallas import tpu as pltpu
from jax.sharding import PartitionSpec as P

MESH = pl.DeviceIdType.MESH
F32 = jnp.float32
BF16 = jnp.bfloat16
EPS = 1e-06
BIAS = 120.0
LN2 = float(np.log(2.0))
IN_MAX = 6.0


class Code:
    def __init__(self, power, top):
        self.power = power
        self.a = (2.0 ** (2.0 * BIAS / power) - 1.0) / top
        self.top = top

    def encode(self, x):
        size = jnp.minimum(jnp.abs(x), self.top)
        size = jnp.exp2((self.power / LN2) * jnp.log(1.0 + self.a * size) - BIAS)
        return jnp.where(x < 0.0, -size, size).astype(BF16)

    def decode(self, code):
        v = code.astype(F32)
        size = jnp.exp2((1.0 / (LN2 * self.power)) * jnp.log(jnp.abs(v)) + BIAS / self.power)
        size = (size - 1.0) * (1.0 / self.a)
        return jnp.where(v < 0.0, -size, size)


FILTER_CODE = Code(30.0, 6.0)
MIXED_CODE = Code(22.0, 1.0)
CONV_CODE = Code(14.0, 768.0)


def split(x):
    high = x.astype(BF16)
    return high, (x - high.astype(F32)).astype(BF16)


def dot3(a, b):
    dot = functools.partial(jnp.dot, preferred_element_type=F32)
    return dot(a[0], b[0]) + (dot(a[0], b[1]) + dot(a[1], b[0]))


def tables(devices, rows):
    levels = devices.bit_length() - 1
    rev = np.array([int(format(e, f"0{levels}b")[::-1], 2) if levels else 0 for e in range(devices)])
    freq = (2 * rev[:, None] + np.arange(2)[None, :]).reshape(-1)
    blocks = 2 * devices
    full = blocks * rows
    turn = 2.0 * np.pi
    ang = turn * ((freq[:, None] * np.arange(devices)[None, :]) % blocks) / blocks
    outer = np.concatenate((np.cos(ang), -np.sin(ang)), 0)
    tw = turn * ((freq[:, None] * np.arange(rows)[None, :]) % full) / full
    ids = np.arange(rows)
    loc = turn * ((ids[:, None] * ids[None, :]) % rows) / rows
    c, s = np.cos(loc), np.sin(loc)
    fwd = np.block([[c, -s], [s, c]])
    inv = np.block([[c, s], [-s, c]])

    def parts(m):
        m = m.astype(np.float32)
        high = m.astype(jnp.bfloat16)
        return np.stack((high, (m - high.astype(np.float32)).astype(jnp.bfloat16)))

    return (
        parts(outer),
        parts(outer.T / full),
        parts(fwd),
        parts(inv),
        np.stack((np.cos(tw), np.sin(tw))).astype(np.float32),
    )


def kernel(
    n, n_ch, channels,
    q_ref, k_ref, v_ref, taps_ref, skip_ref, gain_ref, filt_ref,
    outer_ref, inner_ref, fwd_ref, inv_ref, tw_ref,
    out_ref,
    ext, halo_send, halo_recv, query, mixed, x_send, x_recv, h_send, h_recv, y_send, y_recv,
    work, spec_re, spec_im, sums, sums_recv,
    halo_sems, x_sems, h_sems, y_sems, sum_send, sum_recv,
):
    me, column = lax.axis_index("ctx"), lax.axis_index("ch")
    rows, width = q_ref.shape
    own = width // n
    tiles = width // 128
    per_tile = 128 // own
    ahead = lax.rem(me + 1, n)

    barrier = pltpu.get_barrier_semaphore()

    def greet(i, _):
        pl.semaphore_signal(barrier, inc=1, device_id=(lax.rem(me + i, n), column), device_id_type=MESH)
        return 0

    lax.fori_loop(1, n, greet, 0)
    for i in range(1, n_ch):
        pl.semaphore_signal(barrier, inc=1, device_id=(me, lax.rem(column + i, n_ch)), device_id_type=MESH)

    for i, ref in enumerate((q_ref, k_ref, v_ref)):
        ext[i, 8 : 8 + rows, :] = ref[...].astype(F32)
        halo_send[2 * i : 2 * i + 2, :] = ext[i, 6 + rows : 8 + rows, :]
    halo_send[6:8, :] = jnp.zeros((2, width), F32)

    def code_filter(part):
        def step(i, _):
            cols = pl.ds(pl.multiple_of(i * 128, 128), 128)
            for j in range(2):
                tile = FILTER_CODE.encode(filt_ref[2 * part + j, :, cols].T)
                h_send[part, pl.ds(i * per_tile, per_tile), j] = tile.reshape(per_tile, own, rows)
            return 0

        lax.fori_loop(0, tiles, step, 0)

    def exchange(src, dst, sems):
        def step(i, _):
            to = lax.rem(me + i, n)
            pltpu.make_async_remote_copy(
                src_ref=src.at[to], dst_ref=dst.at[me], send_sem=sems.at[0], recv_sem=sems.at[1],
                device_id=(to, column), device_id_type=MESH,
            ).start()
            return 0

        lax.fori_loop(1, n, step, 0)
        dst[pl.ds(me, 1)] = src[pl.ds(me, 1)]

    def landed(src, dst, sems):
        return pltpu.make_async_remote_copy(
            src_ref=src.at[pl.ds(0, n - 1)], dst_ref=dst.at[pl.ds(0, n - 1)], send_sem=sems.at[0], recv_sem=sems.at[1],
            device_id=(ahead, column), device_id_type=MESH,
        )

    code_filter(0)
    pl.semaphore_wait(barrier, n - 1 + n_ch - 1)
    halo = pltpu.make_async_remote_copy(
        src_ref=halo_send, dst_ref=halo_recv, send_sem=halo_sems.at[0], recv_sem=halo_sems.at[1],
        device_id=(ahead, column), device_id_type=MESH,
    )
    halo.start()
    exchange(h_send.at[0], h_recv.at[0], h_sems.at[0])
    code_filter(1)
    halo.wait()
    inside = jnp.where(me > 0, 1.0, 0.0)
    for i in range(3):
        ext[i, 6:8, :] = halo_recv[2 * i : 2 * i + 2, :] * inside

    def bounds(cols):
        size = [
            sum(jnp.abs(taps_ref[3 * i + lag : 3 * i + lag + 1, cols]) for lag in range(3)) * IN_MAX for i in (1, 2)
        ]
        return jnp.maximum(size[0] * size[1], 1e-30)

    def mix(i, _):
        cols = pl.ds(pl.multiple_of(i * 128, 128), 128)

        def short(which):
            return sum(
                taps_ref[3 * which + lag : 3 * which + lag + 1, cols] * ext[which, 8 - lag : 8 - lag + rows, cols]
                for lag in range(3)
            )

        query[:, cols] = short(0)
        value = short(1) * short(2)
        mixed[:, cols] = value
        code = MIXED_CODE.encode((value / bounds(cols)).T)
        x_send[pl.ds(i * per_tile, per_tile)] = code.reshape(per_tile, own, rows)
        return 0

    lax.fori_loop(0, tiles, mix, 0)
    exchange(x_send, x_recv, x_sems)
    exchange(h_send.at[1], h_recv.at[1], h_sems.at[1])
    landed(x_send, x_recv, x_sems).wait()

    half = 2 * n

    def widen(i, _):
        at = pl.ds(pl.multiple_of(i * own, own), own)
        work[at, :] = MIXED_CODE.decode(x_recv[i])
        return 0

    lax.fori_loop(0, n, widen, 0)

    def over_blocks(c, _):
        x = split(work[pl.ds(c, n, stride=own), :])
        y = dot3((outer_ref[0], outer_ref[1]), x)
        re, im = y[:half], y[half:]
        cos, sin = tw_ref[0], tw_ref[1]
        spec_re[pl.ds(c, half, stride=own), :] = re * cos + im * sin
        spec_im[pl.ds(c, half, stride=own), :] = im * cos - re * sin
        return 0

    lax.fori_loop(0, own, over_blocks, 0)

    def over_rows(at, mat):
        re = split(spec_re[at, :])
        im = split(spec_im[at, :])
        both = tuple(jnp.concatenate((a, b), axis=1) for a, b in zip(re, im))
        return dot3(both, (mat[0], mat[1]))

    step_rows = min(256, half * own)
    steps = half * own // step_rows

    def forward(i, _):
        at = pl.ds(pl.multiple_of(i * step_rows, step_rows), step_rows)
        x = over_rows(at, fwd_ref)
        spec_re[at, :] = x[:, :rows]
        spec_im[at, :] = x[:, rows:]
        return 0

    lax.fori_loop(0, steps, forward, 0)

    for part in range(2):
        landed(h_send.at[part], h_recv.at[part], h_sems.at[part]).wait()

    def multiply(i, _):
        size = 2 * own
        at = pl.ds(pl.multiple_of(i * size, size), size)
        f_re = FILTER_CODE.decode(h_recv[0, i].reshape(size, rows))
        f_im = FILTER_CODE.decode(h_recv[1, i].reshape(size, rows))
        re, im = spec_re[at, :], spec_im[at, :]
        spec_re[at, :] = re * f_re - im * f_im
        spec_im[at, :] = re * f_im + im * f_re
        return 0

    lax.fori_loop(0, n, multiply, 0)

    def backward(i, _):
        at = pl.ds(pl.multiple_of(i * step_rows, step_rows), step_rows)
        x = over_rows(at, inv_ref)
        spec_re[at, :] = x[:, :rows]
        spec_im[at, :] = x[:, rows:]
        return 0

    lax.fori_loop(0, steps, backward, 0)

    def back_over_blocks(c, _):
        re, im = spec_re[pl.ds(c, half, stride=own), :], spec_im[pl.ds(c, half, stride=own), :]
        cos, sin = tw_ref[0], tw_ref[1]
        turned = jnp.concatenate((re * cos - im * sin, im * cos + re * sin), axis=0)
        work[pl.ds(c, n, stride=own), :] = dot3((inner_ref[0], inner_ref[1]), split(turned))
        return 0

    lax.fori_loop(0, own, back_over_blocks, 0)

    def narrow(i, _):
        at = pl.ds(pl.multiple_of(i * own, own), own)
        y_send[i] = CONV_CODE.encode(work[at, :])
        return 0

    lax.fori_loop(0, n, narrow, 0)
    exchange(y_send, y_recv, y_sems)
    landed(y_send, y_recv, y_sems).wait()

    sums[...] = jnp.zeros_like(sums)

    def gate(i, total):
        cols = pl.ds(pl.multiple_of(i * 128, 128), 128)
        conv = CONV_CODE.decode(y_recv[pl.ds(i * per_tile, per_tile)].reshape(128, rows)).T * bounds(cols)
        gated = query[:, cols] * (conv + skip_ref[:, cols] * mixed[:, cols])
        query[:, cols] = gated
        return total + gated * gated

    total = lax.fori_loop(0, tiles, gate, jnp.zeros((rows, 128), F32))
    sums[0:1, :] = jnp.sum(total.T, axis=0, keepdims=True)
    sends = []
    for i in range(1, n_ch):
        copy = pltpu.make_async_remote_copy(
            src_ref=sums, dst_ref=sums_recv.at[i], send_sem=sum_send.at[i], recv_sem=sum_recv.at[i],
            device_id=(me, lax.rem(column + i, n_ch)), device_id_type=MESH,
        )
        copy.start()
        sends.append(copy)
    square = sums[0:1, :]
    for i, copy in enumerate(sends):
        copy.wait()
        square = square + sums_recv[i + 1, 0:1, :]
    scale = lax.rsqrt(square / channels + EPS)
    scale = jnp.broadcast_to(scale, (128, rows)).T

    def finish(i, _):
        cols = pl.ds(pl.multiple_of(i * 128, 128), 128)
        out_ref[:, cols] = (query[:, cols] * scale * gain_ref[:, cols]).astype(BF16)
        return 0

    lax.fori_loop(0, tiles, finish, 0)


def per_device(q_in, k_in, v_in, short_taps, skip_bias, norm_gain, filter_spectrum):
    rows, width = q_in.shape
    n, n_ch = lax.axis_size("ctx"), lax.axis_size("ch")
    own = width // n
    half = 2 * n
    consts = tables(n, rows)
    vmem = pl.BlockSpec(memory_space=pltpu.VMEM)
    dma = pltpu.SemaphoreType.DMA
    return pl.pallas_call(
        functools.partial(kernel, n, n_ch, float(width * n_ch)),
        out_shape=jax.ShapeDtypeStruct((rows, width), BF16),
        in_specs=[vmem] * (7 + len(consts)),
        out_specs=vmem,
        scratch_shapes=[
            pltpu.VMEM((3, rows + 8, width), F32),
            pltpu.VMEM((8, width), F32),
            pltpu.VMEM((8, width), F32),
            pltpu.VMEM((rows, width), F32),
            pltpu.VMEM((rows, width), F32),
            pltpu.VMEM((n, own, rows), BF16),
            pltpu.VMEM((n, own, rows), BF16),
            pltpu.VMEM((2, n, 2, own, rows), BF16),
            pltpu.VMEM((2, n, 2, own, rows), BF16),
            pltpu.VMEM((n, own, rows), BF16),
            pltpu.VMEM((n, own, rows), BF16),
            pltpu.VMEM((n * own, rows), F32),
            pltpu.VMEM((half * own, rows), F32),
            pltpu.VMEM((half * own, rows), F32),
            pltpu.VMEM((8, 128), F32),
            pltpu.VMEM((n_ch, 8, 128), F32),
            dma((2,)),
            dma((2,)),
            dma((2, 2)),
            dma((2,)),
            dma((n_ch,)),
            dma((n_ch,)),
        ],
        compiler_params=pltpu.CompilerParams(
            collective_id=0, has_side_effects=True, vmem_limit_bytes=56 * 2**20
        ),
    )(
        q_in, k_in, v_in,
        short_taps.reshape(-1, width), skip_bias[None], norm_gain[None],
        filter_spectrum.reshape(4, rows, width),
        *(jnp.asarray(c) for c in consts),
    )


def solution(mesh):
    placed = (
        P("ctx", "ch"),
        P("ctx", "ch"),
        P("ctx", "ch"),
        P(None, None, "ch"),
        P("ch"),
        P("ch"),
        P(None, "ctx", None, None, "ch"),
    )
    return jax.shard_map(
        per_device, mesh=mesh, in_specs=placed, out_specs=P("ctx", "ch"), check_vma=False
    )
```

time: 754 us -> 72.3 us (0.10)
  waiting for transfers between devices: 576 us -> 0 us
  starting transfers between devices: 85.6 us -> 0 us
  Pallas kernels: 0 us -> 69 us
  other arithmetic: 47.4 us -> 0 us
  local copies, waits for them, and re-layouts: 16.4 us -> 3.12 us
  matrix products: 10.3 us -> 0 us
  blocking collectives: 8.41 us -> 0 us
    ppermute x13 -> x0, waiting for transfers between devices: 576 us -> none  [the longest x12 575 us: partner_2(): lax.ppermute(value, axis, [(i, i ^ 1 << bit) for i in range(lax.axis_size...]
    ppermute x13 -> x0, starting transfers between devices: 85.6 us -> none  [the longest x12 80.7 us: partner_2(): lax.ppermute(value, axis, [(i, i ^ 1 << bit) for i in range(lax.axis_size...]
    pallas_call x0 -> x1, Pallas kernels: none -> 69 us  [per_device(): pl.pallas_call(functools.partial(kernel, n, n_ch, float(width * n_ch)), o...]
    select_n x12 -> x0, other arithmetic: 16.9 us -> none  [the longest x6 15.7 us: per_device(): jnp.where(upper_side, jnp.stack((diff_real, diff_imag)), state + partner)]
    add x8 -> x0, other arithmetic: 12.8 us -> none  [the longest x5 10.4 us: per_device(): lower_value = jnp.stack((state[0] + part_real, state[1] + part_imag))]
    sub x6 -> x0, other arithmetic: 11.3 us -> none  [rotate(): real_part * cosine - imag_part * sine]
    dot_general x8 -> x0, matrix products: 10.3 us -> none  [product(): return jnp.einsum(form, table, operand, precision=lax.Precision.HIGHEST)]
    unnamed x43 -> x1, local copies, waits for them, and re-layouts: 11.6 us -> 1.67 us
  transfers between devices with their start and end apart: 13 -> 0, of which waited for: 12 -> 0; matrix products, arithmetic and copies ran while one was open for 1% -> 0% of each run, Pallas kernels for 0% -> 0%
where the time goes in v1:
time: 72.3 us; the launch traced here: 72.2 us
  Pallas kernels  69 us (95%)
  local copies, waits for them, and re-layouts  3.12 us (4%)
    pallas_call x1, Pallas kernels, per_device(): pl.pallas_call(functools.partial(kernel, n, n_ch, float(width * n_ch)), o...  69 us
    unnamed x1, local copies, waits for them, and re-layouts  1.67 us

profile of v1, /device:TPU:1, one launch (start us, length us, event | category | flops | bytes accessed | tf_op | source)
XLA Modules:
  0.0 72.2 jit_solution(6564169537354611)
XLA Ops:
  0.0 1.4 %reshape.6.taps_ref = f32[9,1024]{1,0:T(8,128)} reshape(f32[3,3,1024]{2,1,0:T(4,128)} %param.15) | data formatting | bytes 73728 | tf_op jit(solution)/shard_map/reshape | solution.py:339
  1.4 69.0 %shard_map.118 = bf16[128,1024]{1,0:T(8,128)(2,1)} custom-call(bf16[128,1024]{1,0:T(8,128)(2,1)} %q_ref.1, bf16[128,1024]{1,0:T(8,128)(2,1)} %k_ref.1, bf16[128,1024]{1,0:T(8,128)(2,1)} %v_ref.1, f32[9,1024]{1,0:T(8,128)} %reshape.6.taps_ref, f32[1,1024]{1,0:T(1,128)} %bitcast.4, f32[1,1024]{1,0:T(1,128)} %bitcast.5, f32[4,128,1024]{2,1,0:T(8,128)} %bitcast.3, ...), custom_call_target="tpu_custom_call" | custom-call | tf_op jit(solution)/shard_map/pallas_call | solution.py:305
  70.5 1.7 %copy.14 = bf16[128,1024]{1,0:T(8,128)(2,1)} copy(bf16[128,1024]{1,0:T(8,128)(2,1)} %shard_map.118) | data formatting | bytes 524288

commit v2 on v1

v2 whole, which is shorter than its diff:
```python
import functools

import jax
import jax.numpy as jnp
import numpy as np
from jax import lax
from jax.experimental import pallas as pl
from jax.experimental.pallas import tpu as pltpu
from jax.sharding import PartitionSpec as P

MESH = pl.DeviceIdType.MESH
F32 = jnp.float32
BF16 = jnp.bfloat16
EPS = 1e-06
BIAS = 120.0
LN2 = float(np.log(2.0))
IN_MAX = 6.0
GROUPS = 4


class Code:
    def __init__(self, power, top):
        self.power = power
        self.a = (2.0 ** (2.0 * BIAS / power) - 1.0) / top
        self.top = top

    def encode(self, x):
        size = jnp.minimum(jnp.abs(x), self.top)
        size = jnp.exp2((self.power / LN2) * jnp.log(1.0 + self.a * size) - BIAS)
        return jnp.where(x < 0.0, -size, size).astype(BF16)

    def decode(self, code):
        v = code.astype(F32)
        size = jnp.exp2((1.0 / (LN2 * self.power)) * jnp.log(jnp.abs(v)) + BIAS / self.power)
        size = (size - 1.0) * (1.0 / self.a)
        return jnp.where(v < 0.0, -size, size)


FILTER_CODE = Code(30.0, 6.0)
MIXED_CODE = Code(22.0, 1.0)
CONV_CODE = Code(14.0, 768.0)


def split(x):
    high = x.astype(BF16)
    return high, (x - high.astype(F32)).astype(BF16)


def dot(a, b):
    return jnp.dot(a, b, preferred_element_type=F32)


def tables(devices, rows):
    levels = devices.bit_length() - 1
    rev = np.array([int(format(e, f"0{levels}b")[::-1], 2) if levels else 0 for e in range(devices)])
    freq = (2 * rev[:, None] + np.arange(2)[None, :]).reshape(-1)
    blocks = 2 * devices
    full = blocks * rows
    turn = 2.0 * np.pi
    ang = turn * ((freq[:, None] * np.arange(devices)[None, :]) % blocks) / blocks
    outer = np.concatenate((np.cos(ang), -np.sin(ang)), 0)
    tw = turn * ((freq[:, None] * np.arange(rows)[None, :]) % full) / full
    ids = np.arange(rows)
    loc = turn * ((ids[:, None] * ids[None, :]) % rows) / rows
    c, s = np.cos(loc), np.sin(loc)

    def parts(m):
        m = m.astype(np.float32)
        high = m.astype(jnp.bfloat16)
        return high, (m - high.astype(np.float32)).astype(jnp.bfloat16)

    outer_high, outer_low = parts(outer)
    return (
        np.concatenate((outer_high, outer_high, outer_low), 1),
        np.concatenate(parts(outer.T / full), 0),
        np.stack(parts(np.block([[c, -s], [s, c]]))),
        np.stack(parts(np.block([[c, s], [-s, c]]))),
        np.stack((np.cos(tw), np.sin(tw))).astype(np.float32),
    )


def kernel(
    n, n_ch, channels,
    q_hbm, k_hbm, v_hbm, taps_hbm, skip_hbm, gain_hbm, filt_hbm, *rest,
):
    consts_hbm, rest = rest[:5], rest[5:]
    (
        out_ref,
        feats, taps_ref, skip_ref, gain_ref, filt, outer_ref, inner_ref, fwd_ref, inv_ref, tw_ref,
        ext, halo_send, halo_recv, query, mixed, x_send, x_recv, h_send, h_recv, y_send, y_recv,
        work, spec_re, spec_im, stage_high, stage_low, sums, sums_recv,
        in_sems, halo_sems, x_sems, h_send_sems, h_recv_sems, y_sems, sum_send, sum_recv,
    ) = rest
    me, column = lax.axis_index("ctx"), lax.axis_index("ch")
    rows, width = q_hbm.shape
    own = width // n
    part = own // 2
    half_width = width // 2
    tiles = half_width // 128
    per_tile = 128 // part
    blocks = 2 * n
    group = n // GROUPS
    ahead = lax.rem(me + 1, n)

    barrier = pltpu.get_barrier_semaphore()

    def greet(i, _):
        pl.semaphore_signal(barrier, inc=1, device_id=(lax.rem(me + i, n), column), device_id_type=MESH)
        return 0

    for i in range(1, n_ch):
        pl.semaphore_signal(barrier, inc=1, device_id=(me, lax.rem(column + i, n_ch)), device_id_type=MESH)
    lax.fori_loop(1, n, greet, 0)

    moves = [
        (filt_hbm.at[:, :, pl.ds(0, half_width)], filt.at[0]),
        (q_hbm, feats.at[0]),
        (k_hbm, feats.at[1]),
        (v_hbm, feats.at[2]),
        (taps_hbm, taps_ref),
        (filt_hbm.at[:, :, pl.ds(half_width, half_width)], filt.at[1]),
        *zip(consts_hbm, (outer_ref, inner_ref, fwd_ref, inv_ref, tw_ref)),
        (skip_hbm, skip_ref),
        (gain_hbm, gain_ref),
    ]
    loads = [pltpu.make_async_copy(src, dst, in_sems.at[i]) for i, (src, dst) in enumerate(moves)]
    for load in loads:
        load.start()

    def code_filter(h):
        def step(i, _):
            cols = pl.ds(pl.multiple_of(i * 128, 128), 128)
            for j in range(4):
                tile = FILTER_CODE.encode(filt[h, j, :, cols].T.reshape(per_tile, part, rows))
                h_send[h, pl.ds(i * per_tile, per_tile), j * part : (j + 1) * part] = tile
            return 0

        lax.fori_loop(0, tiles, step, 0)

    def send_filter(h):
        def step(i, _):
            to = lax.rem(me + i, n)
            pltpu.make_async_remote_copy(
                src_ref=h_send.at[h, to], dst_ref=h_recv.at[h, me],
                send_sem=h_send_sems.at[h], recv_sem=h_recv_sems.at[h, i // group],
                device_id=(to, column), device_id_type=MESH,
            ).start()
            return 0

        pltpu.make_async_copy(h_send.at[h, me], h_recv.at[h, me], h_recv_sems.at[h, 0]).start()
        lax.fori_loop(1, n, step, 0)

    def exchange(src, dst, sems):
        def step(i, _):
            to = lax.rem(me + i, n)
            pltpu.make_async_remote_copy(
                src_ref=src.at[to], dst_ref=dst.at[me], send_sem=sems.at[0], recv_sem=sems.at[1],
                device_id=(to, column), device_id_type=MESH,
            ).start()
            return 0

        lax.fori_loop(1, n, step, 0)
        dst[pl.ds(me, 1)] = src[pl.ds(me, 1)]

    def of_all(src, dst, send_sem, recv_sem, count):
        return pltpu.make_async_remote_copy(
            src_ref=src.at[pl.ds(0, count)], dst_ref=dst.at[pl.ds(0, count)], send_sem=send_sem, recv_sem=recv_sem,
            device_id=(ahead, column), device_id_type=MESH,
        )

    for load in loads[1:4]:
        load.wait()
    for i in range(3):
        ext[i, 8 : 8 + rows, :] = feats[i].astype(F32)
        halo_send[2 * i : 2 * i + 2, :] = ext[i, 6 + rows : 8 + rows, :]
    halo_send[6:8, :] = jnp.zeros((2, width), F32)
    sums[...] = jnp.zeros_like(sums)
    loads[0].wait()
    code_filter(0)
    pl.semaphore_wait(barrier, n - 1 + n_ch - 1)
    halo = pltpu.make_async_remote_copy(
        src_ref=halo_send, dst_ref=halo_recv, send_sem=halo_sems.at[0], recv_sem=halo_sems.at[1],
        device_id=(ahead, column), device_id_type=MESH,
    )
    halo.start()
    send_filter(0)
    loads[5].wait()
    code_filter(1)
    loads[4].wait()
    halo.wait()
    inside = jnp.where(me > 0, 1.0, 0.0)
    for i in range(3):
        ext[i, 6:8, :] = halo_recv[2 * i : 2 * i + 2, :] * inside

    def bounds(cols):
        size = [sum(jnp.abs(taps_ref[i, lag : lag + 1, cols]) for lag in range(3)) * IN_MAX for i in (1, 2)]
        return jnp.maximum(size[0] * size[1], 1e-30)

    for h in range(2):

        def mix(i, _, h=h):
            cols = pl.ds(pl.multiple_of(h * half_width + i * 128, 128), 128)

            def short(which):
                return sum(
                    taps_ref[which, lag : lag + 1, cols] * ext[which, 8 - lag : 8 - lag + rows, cols]
                    for lag in range(3)
                )

            query[:, cols] = short(0)
            value = short(1) * short(2)
            mixed[:, cols] = value
            code = MIXED_CODE.encode((value / bounds(cols)).T.reshape(per_tile, part, rows))
            x_send[pl.ds(i * per_tile, per_tile), h * part : (h + 1) * part] = code
            return 0

        lax.fori_loop(0, tiles, mix, 0)
    exchange(x_send, x_recv, x_sems)
    send_filter(1)
    for load in loads[6:]:
        load.wait()
    of_all(x_send, x_recv, x_sems.at[0], x_sems.at[1], n - 1).wait()

    def widen(i, _):
        at = pl.ds(pl.multiple_of(i * own, own), own)
        work[at, :] = MIXED_CODE.decode(x_recv[i])
        return 0

    lax.fori_loop(0, n, widen, 0)
    half_rows = blocks * part

    for h in range(2):

        def over_blocks(c, _, h=h):
            x = jnp.concatenate(
                [work[pl.ds(h * part + 2 * c + u, n, stride=own), :] for u in range(2)], axis=1
            )
            high, low = split(x)
            y = dot(outer_ref[...], jnp.concatenate((high, low, high), axis=0))
            cos, sin = tw_ref[0], tw_ref[1]
            for u in range(2):
                re, im = y[:blocks, u * rows : (u + 1) * rows], y[blocks:, u * rows : (u + 1) * rows]
                at = pl.ds(h * half_rows + 2 * c + u, blocks, stride=part)
                spec_re[at, :] = re * cos + im * sin
                spec_im[at, :] = im * cos - re * sin
            return 0

        lax.fori_loop(0, part // 2, over_blocks, 0)

    def over_rows(high, low, mat):
        return dot(high, mat[0]) + (dot(high, mat[1]) + dot(low, mat[0]))

    step_rows = min(256, half_rows)

    def forward(i, _):
        at = pl.ds(pl.multiple_of(i * step_rows, step_rows), step_rows)
        high, low = split(jnp.concatenate((spec_re[at, :], spec_im[at, :]), axis=1))
        x = over_rows(high, low, fwd_ref)
        spec_re[at, :] = x[:, :rows]
        spec_im[at, :] = x[:, rows:]
        return 0

    lax.fori_loop(0, 2 * half_rows // step_rows, forward, 0)

    size = 2 * part
    for h in range(2):

        def backward(g, _, h=h):
            of_all(
                h_send.at[h], h_recv.at[h], h_send_sems.at[h], h_recv_sems.at[h, g], group
            ).wait_recv()

            def place(u):
                e = lax.rem(me - (g * group + u) + n, n)
                return e, pl.ds(pl.multiple_of(h * half_rows + e * size, size), size)

            for u in range(group):
                e, at = place(u)
                f_re = FILTER_CODE.decode(h_recv[h, e, :size])
                f_im = FILTER_CODE.decode(h_recv[h, e, size:])
                re, im = spec_re[at, :], spec_im[at, :]
                high, low = split(jnp.concatenate((re * f_re - im * f_im, re * f_im + im * f_re), axis=1))
                stage_high[u * size : (u + 1) * size, :] = high
                stage_low[u * size : (u + 1) * size, :] = low
            x = over_rows(stage_high[...], stage_low[...], inv_ref)
            for u in range(group):
                _, at = place(u)
                spec_re[at, :] = x[u * size : (u + 1) * size, :rows]
                spec_im[at, :] = x[u * size : (u + 1) * size, rows:]
            return 0

        lax.fori_loop(0, GROUPS, backward, 0)

        def back_over_blocks(c, _, h=h):
            cos, sin = tw_ref[0], tw_ref[1]
            turned = []
            for u in range(2):
                at = pl.ds(h * half_rows + 2 * c + u, blocks, stride=part)
                re, im = spec_re[at, :], spec_im[at, :]
                turned.append(jnp.concatenate((re * cos - im * sin, im * cos + re * sin), axis=0))
            high, low = split(jnp.concatenate(turned, axis=1))
            y = dot(inner_ref[...], high)
            y = y[:n] + (y[n:] + dot(inner_ref[:n, :], low))
            for u in range(2):
                work[pl.ds(2 * c + u, n, stride=part), :] = y[:, u * rows : (u + 1) * rows]
            return 0

        lax.fori_loop(0, part // 2, back_over_blocks, 0)

        def narrow(i, _, h=h):
            at = pl.ds(pl.multiple_of(i * 8 * part, 8 * part), 8 * part)
            y_send[h, pl.ds(i * 8, 8)] = CONV_CODE.encode(work[at, :].reshape(8, part, rows))
            return 0

        lax.fori_loop(0, n // 8, narrow, 0)
        exchange(y_send.at[h], y_recv.at[h], y_sems.at[h])

    total = jnp.zeros((rows, 128), F32)
    for h in range(2):
        of_all(y_send.at[h], y_recv.at[h], y_sems.at[h, 0], y_sems.at[h, 1], n - 1).wait()

        def gate(i, total, h=h):
            cols = pl.ds(pl.multiple_of(h * half_width + i * 128, 128), 128)
            conv = CONV_CODE.decode(y_recv[h, pl.ds(i * per_tile, per_tile)]).reshape(128, rows).T * bounds(cols)
            gated = query[:, cols] * (conv + skip_ref[:, cols] * mixed[:, cols])
            query[:, cols] = gated
            return total + gated * gated

        total = lax.fori_loop(0, tiles, gate, total)
    sums[0:1, :] = jnp.sum(total.T, axis=0, keepdims=True)
    sends = []
    for i in range(1, n_ch):
        copy = pltpu.make_async_remote_copy(
            src_ref=sums, dst_ref=sums_recv.at[i], send_sem=sum_send.at[i], recv_sem=sum_recv.at[i],
            device_id=(me, lax.rem(column + i, n_ch)), device_id_type=MESH,
        )
        copy.start()
        sends.append(copy)
    for h in range(2):
        of_all(h_send.at[h], h_recv.at[h], h_send_sems.at[h], h_recv_sems.at[h, 0], n - 1).wait_send()
    square = sums[0:1, :]
    for i, copy in enumerate(sends):
        copy.wait()
        square = square + sums_recv[i + 1, 0:1, :]
    scale = lax.rsqrt(square / channels + EPS)
    scale = jnp.broadcast_to(scale, (128, rows)).T

    def finish(i, _):
        cols = pl.ds(pl.multiple_of(i * 128, 128), 128)
        out_ref[:, cols] = (query[:, cols] * scale * gain_ref[:, cols]).astype(BF16)
        return 0

    lax.fori_loop(0, 2 * tiles, finish, 0)


def per_device(q_in, k_in, v_in, short_taps, skip_bias, norm_gain, filter_spectrum):
    rows, width = q_in.shape
    n, n_ch = lax.axis_size("ctx"), lax.axis_size("ch")
    own = width // n
    part = own // 2
    blocks = 2 * n
    consts = tables(n, rows)
    anywhere = pl.BlockSpec(memory_space=pl.ANY)
    dma = pltpu.SemaphoreType.DMA
    like = [pltpu.VMEM(c.shape, c.dtype) for c in consts]
    return pl.pallas_call(
        functools.partial(kernel, n, n_ch, float(width * n_ch)),
        out_shape=jax.ShapeDtypeStruct((rows, width), BF16),
        in_specs=[anywhere] * (7 + len(consts)),
        out_specs=pl.BlockSpec(memory_space=pltpu.VMEM),
        scratch_shapes=[
            pltpu.VMEM((3, rows, width), BF16),
            pltpu.VMEM(short_taps.shape, F32),
            pltpu.VMEM((1, width), F32),
            pltpu.VMEM((1, width), F32),
            pltpu.VMEM((2, 4, rows, width // 2), F32),
            *like,
            pltpu.VMEM((3, rows + 8, width), F32),
            pltpu.VMEM((8, width), F32),
            pltpu.VMEM((8, width), F32),
            pltpu.VMEM((rows, width), F32),
            pltpu.VMEM((rows, width), F32),
            pltpu.VMEM((n, own, rows), BF16),
            pltpu.VMEM((n, own, rows), BF16),
            pltpu.VMEM((2, n, 4 * part, rows), BF16),
            pltpu.VMEM((2, n, 4 * part, rows), BF16),
            pltpu.VMEM((2, n, part, rows), BF16),
            pltpu.VMEM((2, n, part, rows), BF16),
            pltpu.VMEM((n * own, rows), F32),
            pltpu.VMEM((blocks * own, rows), F32),
            pltpu.VMEM((blocks * own, rows), F32),
            pltpu.VMEM((n // GROUPS * own, 2 * rows), BF16),
            pltpu.VMEM((n // GROUPS * own, 2 * rows), BF16),
            pltpu.VMEM((8, 128), F32),
            pltpu.VMEM((n_ch, 8, 128), F32),
            dma((13,)),
            dma((2,)),
            dma((2,)),
            dma((2,)),
            dma((2, GROUPS)),
            dma((2, 2)),
            dma((n_ch,)),
            dma((n_ch,)),
        ],
        compiler_params=pltpu.CompilerParams(
            collective_id=0, has_side_effects=True, vmem_limit_bytes=56 * 2**20
        ),
    )(
        q_in, k_in, v_in, short_taps, skip_bias[None], norm_gain[None],
        filter_spectrum.reshape(4, rows, width),
        *(jnp.asarray(c) for c in consts),
    )


def solution(mesh):
    placed = (
        P("ctx", "ch"),
        P("ctx", "ch"),
        P("ctx", "ch"),
        P(None, None, "ch"),
        P("ch"),
        P("ch"),
        P(None, "ctx", None, None, "ch"),
    )
    return jax.shard_map(
        per_device, mesh=mesh, in_specs=placed, out_specs=P("ctx", "ch"), check_vma=False
    )
```

time: 72.3 us -> 59 us (0.82)
  Pallas kernels: 69 us -> 57.2 us
  local copies, waits for them, and re-layouts: 3.12 us -> 1.67 us
    pallas_call x1, Pallas kernels: 69 us -> 57.2 us  [per_device(): pl.pallas_call(functools.partial(kernel, n, n_ch, float(width * n_ch)), o...]
    reshape x1 -> x0, local copies, waits for them, and re-layouts: 1.45 us -> none  [per_device(): short_taps.reshape(-1, width)]
where the time goes in v2:
time: 59 us; the launch traced here: 58.9 us
  Pallas kernels  57.2 us (97%)
  local copies, waits for them, and re-layouts  1.67 us (3%)
    pallas_call x1, Pallas kernels, per_device(): pl.pallas_call(functools.partial(kernel, n, n_ch, float(width * n_ch)), o...  57.2 us
    unnamed x1, local copies, waits for them, and re-layouts  1.67 us

profile of v2, /device:TPU:1, one launch (start us, length us, event | category | flops | bytes accessed | tf_op | source)
XLA Modules:
  0.0 58.9 jit_solution(1499035596698251831)
XLA Ops:
  0.0 57.2 %shard_map.118 = bf16[128,1024]{1,0:T(8,128)(2,1)} custom-call(bf16[128,1024]{1,0:T(8,128)(2,1)} %q_hbm.1, bf16[128,1024]{1,0:T(8,128)(2,1)} %k_hbm.1, bf16[128,1024]{1,0:T(8,128)(2,1)} %v_hbm.1, f32[3,3,1024]{2,1,0:T(4,128)} %taps_hbm.1, f32[1,1024]{1,0:T(1,128)} %bitcast.4, f32[1,1024]{1,0:T(1,128)} %bitcast.5, f32[4,128,1024]{2,1,0:T(8,128)} %bitcast.3, ...), custom_call_target="tpu_custom_call" | custom-call | tf_op jit(solution)/shard_map/pallas_call | solution.py:366
  57.2 1.7 %copy.14 = bf16[128,1024]{1,0:T(8,128)(2,1)} copy(bf16[128,1024]{1,0:T(8,128)(2,1)} %shard_map.118) | data formatting | bytes 524288

commit v3 on v2

--- a/solution.py
+++ b/solution.py
@@ -12,9 +12,10 @@
 F32 = jnp.float32
 BF16 = jnp.bfloat16
 EPS = 1e-06
-BIAS = 120.0
+BIAS = 125.0
 LN2 = float(np.log(2.0))
 IN_MAX = 6.0
+PARTS = 4
 GROUPS = 4
 
 
@@ -37,8 +38,8 @@
 
 
 FILTER_CODE = Code(30.0, 6.0)
-MIXED_CODE = Code(22.0, 1.0)
-CONV_CODE = Code(14.0, 768.0)
+MIXED_CODE = Code(15.0, 1.0)
+CONV_CODE = Code(10.5, 768.0)
 
 
 def split(x):
@@ -94,9 +95,9 @@
     me, column = lax.axis_index("ctx"), lax.axis_index("ch")
     rows, width = q_hbm.shape
     own = width // n
-    part = own // 2
-    half_width = width // 2
-    tiles = half_width // 128
+    part = own // PARTS
+    part_width = width // PARTS
+    tiles = part_width // 128
     per_tile = 128 // part
     blocks = 2 * n
     group = n // GROUPS
@@ -113,12 +114,11 @@
     lax.fori_loop(1, n, greet, 0)
 
     moves = [
-        (filt_hbm.at[:, :, pl.ds(0, half_width)], filt.at[0]),
+        *((filt_hbm.at[:, :, pl.ds(h * part_width, part_width)], filt.at[h]) for h in range(PARTS)),
         (q_hbm, feats.at[0]),
         (k_hbm, feats.at[1]),
         (v_hbm, feats.at[2]),
         (taps_hbm, taps_ref),
-        (filt_hbm.at[:, :, pl.ds(half_width, half_width)], filt.at[1]),
         *zip(consts_hbm, (outer_ref, inner_ref, fwd_ref, inv_ref, tw_ref)),
         (skip_hbm, skip_ref),
         (gain_hbm, gain_ref),
@@ -168,7 +168,7 @@
             device_id=(ahead, column), device_id_type=MESH,
         )
 
-    for load in loads[1:4]:
+    for load in loads[PARTS : PARTS + 3]:
         load.wait()
     for i in range(3):
         ext[i, 8 : 8 + rows, :] = feats[i].astype(F32)
@@ -184,9 +184,10 @@
     )
     halo.start()
     send_filter(0)
-    loads[5].wait()
-    code_filter(1)
-    loads[4].wait()
+    for h in range(1, PARTS):
+        loads[h].wait()
+        code_filter(h)
+    loads[PARTS + 3].wait()
     halo.wait()
     inside = jnp.where(me > 0, 1.0, 0.0)
     for i in range(3):
@@ -196,10 +197,10 @@
         size = [sum(jnp.abs(taps_ref[i, lag : lag + 1, cols]) for lag in range(3)) * IN_MAX for i in (1, 2)]
         return jnp.maximum(size[0] * size[1], 1e-30)
 
-    for h in range(2):
+    for h in range(PARTS):
 
         def mix(i, _, h=h):
-            cols = pl.ds(pl.multiple_of(h * half_width + i * 128, 128), 128)
+            cols = pl.ds(pl.multiple_of(h * part_width + i * 128, 128), 128)
 
             def short(which):
                 return sum(
@@ -217,9 +218,11 @@
         lax.fori_loop(0, tiles, mix, 0)
     exchange(x_send, x_recv, x_sems)
     send_filter(1)
-    for load in loads[6:]:
+    for load in loads[PARTS + 4 :]:
         load.wait()
     of_all(x_send, x_recv, x_sems.at[0], x_sems.at[1], n - 1).wait()
+    for h in range(2, PARTS):
+        send_filter(h)
 
     def widen(i, _):
         at = pl.ds(pl.multiple_of(i * own, own), own)
@@ -227,9 +230,9 @@
         return 0
 
     lax.fori_loop(0, n, widen, 0)
-    half_rows = blocks * part
-
-    for h in range(2):
+    part_rows = blocks * part
+
+    for h in range(PARTS):
 
         def over_blocks(c, _, h=h):
             x = jnp.concatenate(
@@ -240,7 +243,7 @@
             cos, sin = tw_ref[0], tw_ref[1]
             for u in range(2):
                 re, im = y[:blocks, u * rows : (u + 1) * rows], y[blocks:, u * rows : (u + 1) * rows]
-                at = pl.ds(h * half_rows + 2 * c + u, blocks, stride=part)
+                at = pl.ds(h * part_rows + 2 * c + u, blocks, stride=part)
                 spec_re[at, :] = re * cos + im * sin
                 spec_im[at, :] = im * cos - re * sin
             return 0
@@ -250,7 +253,7 @@
     def over_rows(high, low, mat):
         return dot(high, mat[0]) + (dot(high, mat[1]) + dot(low, mat[0]))
 
-    step_rows = min(256, half_rows)
+    step_rows = min(256, part_rows)
 
     def forward(i, _):
         at = pl.ds(pl.multiple_of(i * step_rows, step_rows), step_rows)
@@ -260,10 +263,10 @@
         spec_im[at, :] = x[:, rows:]
         return 0
 
-    lax.fori_loop(0, 2 * half_rows // step_rows, forward, 0)
+    lax.fori_loop(0, PARTS * part_rows // step_rows, forward, 0)
 
     size = 2 * part
-    for h in range(2):
+    for h in range(PARTS):
 
         def backward(g, _, h=h):
             of_all(
@@ -272,7 +275,7 @@
 
             def place(u):
                 e = lax.rem(me - (g * group + u) + n, n)
-                return e, pl.ds(pl.multiple_of(h * half_rows + e * size, size), size)
+                return e, pl.ds(pl.multiple_of(h * part_rows + e * size, size), size)
 
             for u in range(group):
                 e, at = place(u)
@@ -295,7 +298,7 @@
             cos, sin = tw_ref[0], tw_ref[1]
             turned = []
             for u in range(2):
-                at = pl.ds(h * half_rows + 2 * c + u, blocks, stride=part)
+                at = pl.ds(h * part_rows + 2 * c + u, blocks, stride=part)
                 re, im = spec_re[at, :], spec_im[at, :]
                 turned.append(jnp.concatenate((re * cos - im * sin, im * cos + re * sin), axis=0))
             high, low = split(jnp.concatenate(turned, axis=1))
@@ -316,11 +319,11 @@
         exchange(y_send.at[h], y_recv.at[h], y_sems.at[h])
 
     total = jnp.zeros((rows, 128), F32)
-    for h in range(2):
+    for h in range(PARTS):
         of_all(y_send.at[h], y_recv.at[h], y_sems.at[h, 0], y_sems.at[h, 1], n - 1).wait()
 
         def gate(i, total, h=h):
-            cols = pl.ds(pl.multiple_of(h * half_width + i * 128, 128), 128)
+            cols = pl.ds(pl.multiple_of(h * part_width + i * 128, 128), 128)
             conv = CONV_CODE.decode(y_recv[h, pl.ds(i * per_tile, per_tile)]).reshape(128, rows).T * bounds(cols)
             gated = query[:, cols] * (conv + skip_ref[:, cols] * mixed[:, cols])
             query[:, cols] = gated
@@ -336,7 +339,7 @@
         )
         copy.start()
         sends.append(copy)
-    for h in range(2):
+    for h in range(PARTS):
         of_all(h_send.at[h], h_recv.at[h], h_send_sems.at[h], h_recv_sems.at[h, 0], n - 1).wait_send()
     square = sums[0:1, :]
     for i, copy in enumerate(sends):
@@ -350,14 +353,14 @@
         out_ref[:, cols] = (query[:, cols] * scale * gain_ref[:, cols]).astype(BF16)
         return 0
 
-    lax.fori_loop(0, 2 * tiles, finish, 0)
+    lax.fori_loop(0, PARTS * tiles, finish, 0)
 
 
 def per_device(q_in, k_in, v_in, short_taps, skip_bias, norm_gain, filter_spectrum):
     rows, width = q_in.shape
     n, n_ch = lax.axis_size("ctx"), lax.axis_size("ch")
     own = width // n
-    part = own // 2
+    part = own // PARTS
     blocks = 2 * n
     consts = tables(n, rows)
     anywhere = pl.BlockSpec(memory_space=pl.ANY)
@@ -373,7 +376,7 @@
             pltpu.VMEM(short_taps.shape, F32),
             pltpu.VMEM((1, width), F32),
             pltpu.VMEM((1, width), F32),
-            pltpu.VMEM((2, 4, rows, width // 2), F32),
+            pltpu.VMEM((PARTS, 4, rows, width // PARTS), F32),
             *like,
             pltpu.VMEM((3, rows + 8, width), F32),
             pltpu.VMEM((8, width), F32),
@@ -382,23 +385,23 @@
             pltpu.VMEM((rows, width), F32),
             pltpu.VMEM((n, own, rows), BF16),
             pltpu.VMEM((n, own, rows), BF16),
-            pltpu.VMEM((2, n, 4 * part, rows), BF16),
-            pltpu.VMEM((2, n, 4 * part, rows), BF16),
-            pltpu.VMEM((2, n, part, rows), BF16),
-            pltpu.VMEM((2, n, part, rows), BF16),
+            pltpu.VMEM((PARTS, n, 4 * part, rows), BF16),
+            pltpu.VMEM((PARTS, n, 4 * part, rows), BF16),
+            pltpu.VMEM((PARTS, n, part, rows), BF16),
+            pltpu.VMEM((PARTS, n, part, rows), BF16),
             pltpu.VMEM((n * own, rows), F32),
             pltpu.VMEM((blocks * own, rows), F32),
             pltpu.VMEM((blocks * own, rows), F32),
-            pltpu.VMEM((n // GROUPS * own, 2 * rows), BF16),
-            pltpu.VMEM((n // GROUPS * own, 2 * rows), BF16),
+            pltpu.VMEM((n // GROUPS * 2 * part, 2 * rows), BF16),
+            pltpu.VMEM((n // GROUPS * 2 * part, 2 * rows), BF16),
             pltpu.VMEM((8, 128), F32),
             pltpu.VMEM((n_ch, 8, 128), F32),
-            dma((13,)),
+            dma((11 + PARTS,)),
             dma((2,)),
             dma((2,)),
-            dma((2,)),
-            dma((2, GROUPS)),
-            dma((2, 2)),
+            dma((PARTS,)),
+            dma((PARTS, GROUPS)),
+            dma((PARTS, 2)),
             dma((n_ch,)),
             dma((n_ch,)),
         ],

time: 59 us -> 58.3 us (0.988)
  Pallas kernels: 57.2 us -> 56.5 us
    pallas_call x1, Pallas kernels: 57.2 us -> 56.5 us  [per_device(): pl.pallas_call(functools.partial(kernel, n, n_ch, float(width * n_ch)), o...]
where the time goes in v3:
time: 58.3 us; the launch traced here: 58.2 us
  Pallas kernels  56.5 us (97%)
  local copies, waits for them, and re-layouts  1.67 us (3%)
    pallas_call x1, Pallas kernels, per_device(): pl.pallas_call(functools.partial(kernel, n, n_ch, float(width * n_ch)), o...  56.5 us
    unnamed x1, local copies, waits for them, and re-layouts  1.67 us

profile of v3, /device:TPU:1, one launch (start us, length us, event | category | flops | bytes accessed | tf_op | source)
XLA Modules:
  0.0 58.2 jit_solution(7738042772773340221)
XLA Ops:
  0.0 56.5 %shard_map.118 = bf16[128,1024]{1,0:T(8,128)(2,1)} custom-call(bf16[128,1024]{1,0:T(8,128)(2,1)} %q_hbm.1, bf16[128,1024]{1,0:T(8,128)(2,1)} %k_hbm.1, bf16[128,1024]{1,0:T(8,128)(2,1)} %v_hbm.1, f32[3,3,1024]{2,1,0:T(4,128)} %taps_hbm.1, f32[1,1024]{1,0:T(1,128)} %bitcast.4, f32[1,1024]{1,0:T(1,128)} %bitcast.5, f32[4,128,1024]{2,1,0:T(8,128)} %bitcast.3, ...), custom_call_target="tpu_custom_call" | custom-call | tf_op jit(solution)/shard_map/pallas_call | solution.py:369
  56.5 1.7 %copy.14 = bf16[128,1024]{1,0:T(8,128)(2,1)} copy(bf16[128,1024]{1,0:T(8,128)(2,1)} %shard_map.118) | data formatting | bytes 524288

commit v4 on v3

--- a/solution.py
+++ b/solution.py
@@ -20,26 +20,34 @@
 
 
 class Code:
-    def __init__(self, power, top):
-        self.power = power
-        self.a = (2.0 ** (2.0 * BIAS / power) - 1.0) / top
-        self.top = top
+    def __init__(self, power, top, knee=None, tail=1.0):
+        self.power, self.top, self.tail = power, top, tail
+        self.knee = top if knee is None else knee
+        self.turn = 2.0 * BIAS - tail * float(np.log2(top / self.knee))
+        self.a = (2.0 ** (self.turn / power) - 1.0) / self.knee
 
     def encode(self, x):
         size = jnp.minimum(jnp.abs(x), self.top)
-        size = jnp.exp2((self.power / LN2) * jnp.log(1.0 + self.a * size) - BIAS)
-        return jnp.where(x < 0.0, -size, size).astype(BF16)
+        inner = jnp.minimum(size, self.knee)
+        code = (self.power / LN2) * jnp.log(1.0 + self.a * inner) - BIAS
+        if self.knee < self.top:
+            code = code + (self.tail / LN2) * jnp.log(jnp.maximum(size * (1.0 / self.knee), 1.0))
+        code = jnp.exp2(code)
+        return jnp.where(x < 0.0, -code, code).astype(BF16)
 
     def decode(self, code):
         v = code.astype(F32)
-        size = jnp.exp2((1.0 / (LN2 * self.power)) * jnp.log(jnp.abs(v)) + BIAS / self.power)
-        size = (size - 1.0) * (1.0 / self.a)
-        return jnp.where(v < 0.0, -size, size)
+        size = (1.0 / LN2) * jnp.log(jnp.abs(v)) + BIAS
+        inner = jnp.minimum(size, self.turn) if self.knee < self.top else size
+        x = (jnp.exp2((1.0 / self.power) * inner) - 1.0) * (1.0 / self.a)
+        if self.knee < self.top:
+            x = x * jnp.exp2((1.0 / self.tail) * (size - inner))
+        return jnp.where(v < 0.0, -x, x)
 
 
 FILTER_CODE = Code(30.0, 6.0)
-MIXED_CODE = Code(15.0, 1.0)
-CONV_CODE = Code(10.5, 768.0)
+MIXED_CODE = Code(24.0, 1.0)
+CONV_CODE = Code(15.4, 768.0, 4.0, 4.0)
 
 
 def split(x):
@@ -89,8 +97,8 @@
         out_ref,
         feats, taps_ref, skip_ref, gain_ref, filt, outer_ref, inner_ref, fwd_ref, inv_ref, tw_ref,
         ext, halo_send, halo_recv, query, mixed, x_send, x_recv, h_send, h_recv, y_send, y_recv,
-        work, spec_re, spec_im, stage_high, stage_low, sums, sums_recv,
-        in_sems, halo_sems, x_sems, h_send_sems, h_recv_sems, y_sems, sum_send, sum_recv,
+        work, back, peaks, scale_send, scale_recv, spec_re, spec_im, stage_high, stage_low, sums, sums_recv,
+        in_sems, halo_sems, scale_sems, x_sems, h_send_sems, h_recv_sems, y_sems, sum_send, sum_recv,
     ) = rest
     me, column = lax.axis_index("ctx"), lax.axis_index("ch")
     rows, width = q_hbm.shape
@@ -130,9 +138,10 @@
     def code_filter(h):
         def step(i, _):
             cols = pl.ds(pl.multiple_of(i * 128, 128), 128)
-            for j in range(4):
-                tile = FILTER_CODE.encode(filt[h, j, :, cols].T.reshape(per_tile, part, rows))
-                h_send[h, pl.ds(i * per_tile, per_tile), j * part : (j + 1) * part] = tile
+            tiles_of = [
+                FILTER_CODE.encode(filt[h, j, :, cols].T.reshape(per_tile, part, rows)) for j in range(4)
+            ]
+            h_send[h, pl.ds(i * per_tile, per_tile)] = jnp.concatenate(tiles_of, axis=1)
             return 0
 
         lax.fori_loop(0, tiles, step, 0)
@@ -174,6 +183,8 @@
         ext[i, 8 : 8 + rows, :] = feats[i].astype(F32)
         halo_send[2 * i : 2 * i + 2, :] = ext[i, 6 + rows : 8 + rows, :]
     halo_send[6:8, :] = jnp.zeros((2, width), F32)
+    for i in (1, 2):
+        peaks[i : i + 1, :] = jnp.max(jnp.abs(ext[i, 8 : 8 + rows, :]), axis=0, keepdims=True)
     sums[...] = jnp.zeros_like(sums)
     loads[0].wait()
     code_filter(0)
@@ -184,54 +195,95 @@
     )
     halo.start()
     send_filter(0)
-    for h in range(1, PARTS):
-        loads[h].wait()
-        code_filter(h)
+    loads[1].wait()
+    code_filter(1)
     loads[PARTS + 3].wait()
     halo.wait()
     inside = jnp.where(me > 0, 1.0, 0.0)
     for i in range(3):
         ext[i, 6:8, :] = halo_recv[2 * i : 2 * i + 2, :] * inside
 
+    highest = [
+        jnp.max(jnp.maximum(peaks[i : i + 1, :], jnp.max(jnp.abs(ext[i, 6:8, :]), axis=0, keepdims=True)), axis=1, keepdims=True)
+        for i in (1, 2)
+    ]
+    bound = jnp.maximum(highest[0] * highest[1] * (1.0 / IN_MAX**2), 1e-30)
+    scale_send[...] = jnp.broadcast_to(bound, (1, 128))
+
     def bounds(cols):
         size = [sum(jnp.abs(taps_ref[i, lag : lag + 1, cols]) for lag in range(3)) * IN_MAX for i in (1, 2)]
         return jnp.maximum(size[0] * size[1], 1e-30)
 
-    for h in range(PARTS):
-
-        def mix(i, _, h=h):
-            cols = pl.ds(pl.multiple_of(h * part_width + i * 128, 128), 128)
-
-            def short(which):
-                return sum(
-                    taps_ref[which, lag : lag + 1, cols] * ext[which, 8 - lag : 8 - lag + rows, cols]
-                    for lag in range(3)
-                )
-
-            query[:, cols] = short(0)
-            value = short(1) * short(2)
+    def short(which, cols):
+        return sum(
+            taps_ref[which, lag : lag + 1, cols] * ext[which, 8 - lag : 8 - lag + rows, cols] for lag in range(3)
+        )
+
+    def columns(h, i):
+        return pl.ds(pl.multiple_of(h * part_width + i * 128, 128), 128)
+
+    def mix(i, _):
+        codes = []
+        for h in range(PARTS):
+            cols = columns(h, i)
+            value = short(1, cols) * short(2, cols)
             mixed[:, cols] = value
-            code = MIXED_CODE.encode((value / bounds(cols)).T.reshape(per_tile, part, rows))
-            x_send[pl.ds(i * per_tile, per_tile), h * part : (h + 1) * part] = code
-            return 0
-
-        lax.fori_loop(0, tiles, mix, 0)
-    exchange(x_send, x_recv, x_sems)
+            value = (value / bounds(cols)) * (1.0 / scale_send[...])
+            codes.append(MIXED_CODE.encode(value.T.reshape(per_tile, part, rows)))
+        x_send[pl.ds(i * per_tile, per_tile)] = jnp.concatenate(codes, axis=1)
+        return 0
+
+    lax.fori_loop(0, tiles, mix, 0)
+
+    def send_mixed(i, _):
+        to = lax.rem(me + i, n)
+        for src, dst, sems in ((scale_send, scale_recv, scale_sems), (x_send.at[to], x_recv, x_sems)):
+            pltpu.make_async_remote_copy(
+                src_ref=src, dst_ref=dst.at[me], send_sem=sems.at[0], recv_sem=sems.at[1],
+                device_id=(to, column), device_id_type=MESH,
+            ).start()
+        return 0
+
+    lax.fori_loop(1, n, send_mixed, 0)
+    x_recv[pl.ds(me, 1)] = x_send[pl.ds(me, 1)]
+    scale_recv[pl.ds(me, 1)] = scale_send[...].reshape(1, 1, 128)
     send_filter(1)
+    for h in range(2, PARTS):
+        loads[h].wait()
+        code_filter(h)
+
+    def gates(i, _):
+        for h in range(PARTS):
+            cols = columns(h, i)
+            query[:, cols] = short(0, cols)
+        return 0
+
+    lax.fori_loop(0, tiles, gates, 0)
     for load in loads[PARTS + 4 :]:
         load.wait()
     of_all(x_send, x_recv, x_sems.at[0], x_sems.at[1], n - 1).wait()
+    of_all(scale_recv, scale_recv, scale_sems.at[0], scale_sems.at[1], n - 1).wait()
     for h in range(2, PARTS):
         send_filter(h)
 
+    unit = jnp.max(scale_recv[...], axis=0)
+    scale_send[...] = unit
+
     def widen(i, _):
-        at = pl.ds(pl.multiple_of(i * own, own), own)
-        work[at, :] = MIXED_CODE.decode(x_recv[i])
+        at = pl.ds(pl.multiple_of(i * 8 * own, 8 * own), 8 * own)
+        x = MIXED_CODE.decode(x_recv[pl.ds(i * 8, 8)]) * (scale_recv[pl.ds(i * 8, 8)] / unit)
+        work[at, :] = x.reshape(8 * own, rows)
         return 0
 
-    lax.fori_loop(0, n, widen, 0)
+    lax.fori_loop(0, n // 8, widen, 0)
     part_rows = blocks * part
 
+    def over_rows(high, low, mat):
+        return dot(high, mat[0]) + (dot(high, mat[1]) + dot(low, mat[0]))
+
+    step_rows = min(256, part_rows)
+
+    size = 2 * part
     for h in range(PARTS):
 
         def over_blocks(c, _, h=h):
@@ -248,25 +300,18 @@
                 spec_im[at, :] = im * cos - re * sin
             return 0
 
-        lax.fori_loop(0, part // 2, over_blocks, 0)
-
-    def over_rows(high, low, mat):
-        return dot(high, mat[0]) + (dot(high, mat[1]) + dot(low, mat[0]))
-
-    step_rows = min(256, part_rows)
-
-    def forward(i, _):
-        at = pl.ds(pl.multiple_of(i * step_rows, step_rows), step_rows)
-        high, low = split(jnp.concatenate((spec_re[at, :], spec_im[at, :]), axis=1))
-        x = over_rows(high, low, fwd_ref)
-        spec_re[at, :] = x[:, :rows]
-        spec_im[at, :] = x[:, rows:]
-        return 0
-
-    lax.fori_loop(0, PARTS * part_rows // step_rows, forward, 0)
-
-    size = 2 * part
-    for h in range(PARTS):
+        for c in range(part // 2):
+            over_blocks(c, 0)
+
+        def forward(i, _, h=h):
+            at = pl.ds(pl.multiple_of(h * part_rows + i * step_rows, step_rows), step_rows)
+            high, low = split(jnp.concatenate((spec_re[at, :], spec_im[at, :]), axis=1))
+            x = over_rows(high, low, fwd_ref)
+            spec_re[at, :] = x[:, :rows]
+            spec_im[at, :] = x[:, rows:]
+            return 0
+
+        lax.fori_loop(0, part_rows // step_rows, forward, 0)
 
         def backward(g, _, h=h):
             of_all(
@@ -279,8 +324,8 @@
 
             for u in range(group):
                 e, at = place(u)
-                f_re = FILTER_CODE.decode(h_recv[h, e, :size])
-                f_im = FILTER_CODE.decode(h_recv[h, e, size:])
+                f = FILTER_CODE.decode(h_recv[h, e])
+                f_re, f_im = f[:size], f[size:]
                 re, im = spec_re[at, :], spec_im[at, :]
                 high, low = split(jnp.concatenate((re * f_re - im * f_im, re * f_im + im * f_re), axis=1))
                 stage_high[u * size : (u + 1) * size, :] = high
@@ -305,17 +350,19 @@
             y = dot(inner_ref[...], high)
             y = y[:n] + (y[n:] + dot(inner_ref[:n, :], low))
             for u in range(2):
-                work[pl.ds(2 * c + u, n, stride=part), :] = y[:, u * rows : (u + 1) * rows]
-            return 0
-
-        lax.fori_loop(0, part // 2, back_over_blocks, 0)
+                back[pl.ds(2 * c + u, n, stride=part), :] = y[:, u * rows : (u + 1) * rows]
+            return 0
+
+        for c in range(part // 2):
+            back_over_blocks(c, 0)
 
         def narrow(i, _, h=h):
             at = pl.ds(pl.multiple_of(i * 8 * part, 8 * part), 8 * part)
-            y_send[h, pl.ds(i * 8, 8)] = CONV_CODE.encode(work[at, :].reshape(8, part, rows))
-            return 0
-
-        lax.fori_loop(0, n // 8, narrow, 0)
+            y_send[h, pl.ds(i * 8, 8)] = CONV_CODE.encode(back[at, :].reshape(8, part, rows))
+            return 0
+
+        for i in range(n // 8):
+            narrow(i, 0)
         exchange(y_send.at[h], y_recv.at[h], y_sems.at[h])
 
     total = jnp.zeros((rows, 128), F32)
@@ -324,12 +371,14 @@
 
         def gate(i, total, h=h):
             cols = pl.ds(pl.multiple_of(h * part_width + i * 128, 128), 128)
-            conv = CONV_CODE.decode(y_recv[h, pl.ds(i * per_tile, per_tile)]).reshape(128, rows).T * bounds(cols)
+            conv = CONV_CODE.decode(y_recv[h, pl.ds(i * per_tile, per_tile)]).reshape(128, rows).T
+            conv = conv * (bounds(cols) * scale_send[...])
             gated = query[:, cols] * (conv + skip_ref[:, cols] * mixed[:, cols])
             query[:, cols] = gated
             return total + gated * gated
 
-        total = lax.fori_loop(0, tiles, gate, total)
+        for i in range(tiles):
+            total = gate(i, total)
     sums[0:1, :] = jnp.sum(total.T, axis=0, keepdims=True)
     sends = []
     for i in range(1, n_ch):
@@ -341,6 +390,7 @@
         sends.append(copy)
     for h in range(PARTS):
         of_all(h_send.at[h], h_recv.at[h], h_send_sems.at[h], h_recv_sems.at[h, 0], n - 1).wait_send()
+    query[...] = query[...] * gain_ref[...]
     square = sums[0:1, :]
     for i, copy in enumerate(sends):
         copy.wait()
@@ -348,12 +398,9 @@
     scale = lax.rsqrt(square / channels + EPS)
     scale = jnp.broadcast_to(scale, (128, rows)).T
 
-    def finish(i, _):
-        cols = pl.ds(pl.multiple_of(i * 128, 128), 128)
-        out_ref[:, cols] = (query[:, cols] * scale * gain_ref[:, cols]).astype(BF16)
-        return 0
-
-    lax.fori_loop(0, PARTS * tiles, finish, 0)
+    for i in range(PARTS * tiles):
+        cols = pl.ds(i * 128, 128)
+        out_ref[:, cols] = (query[:, cols] * scale).astype(BF16)
 
 
 def per_device(q_in, k_in, v_in, short_taps, skip_bias, norm_gain, filter_spectrum):
@@ -368,7 +415,7 @@
     like = [pltpu.VMEM(c.shape, c.dtype) for c in consts]
     return pl.pallas_call(
         functools.partial(kernel, n, n_ch, float(width * n_ch)),
-        out_shape=jax.ShapeDtypeStruct((rows, width), BF16),
+        out_shape=pltpu.VMEM((rows, width), BF16),
         in_specs=[anywhere] * (7 + len(consts)),
         out_specs=pl.BlockSpec(memory_space=pltpu.VMEM),
         scratch_shapes=[
@@ -390,6 +437,10 @@
             pltpu.VMEM((PARTS, n, part, rows), BF16),
             pltpu.VMEM((PARTS, n, part, rows), BF16),
             pltpu.VMEM((n * own, rows), F32),
+            pltpu.VMEM((n * part, rows), F32),
+            pltpu.VMEM((8, width), F32),
+            pltpu.VMEM((1, 128), F32),
+            pltpu.VMEM((n, 1, 128), F32),
             pltpu.VMEM((blocks * own, rows), F32),
             pltpu.VMEM((blocks * own, rows), F32),
             pltpu.VMEM((n // GROUPS * 2 * part, 2 * rows), BF16),
@@ -397,6 +448,7 @@
             pltpu.VMEM((8, 128), F32),
             pltpu.VMEM((n_ch, 8, 128), F32),
             dma((11 + PARTS,)),
+            dma((2,)),
             dma((2,)),
             dma((2,)),
             dma((PARTS,)),

time: 58.3 us -> 57 us (0.978)
  local copies, waits for them, and re-layouts: 1.67 us -> 0.71 us
    unnamed x1, local copies, waits for them, and re-layouts: 1.67 us -> 0.71 us
where the time goes in v4:
time: 57 us; the launch traced here: 56.9 us
  Pallas kernels  56.2 us (99%)
  local copies, waits for them, and re-layouts  0.71 us (1%)
    pallas_call x1, Pallas kernels, per_device(): pl.pallas_call(functools.partial(kernel, n, n_ch, float(width * n_ch)), o...  56.2 us

profile of v4, /device:TPU:1, one launch (start us, length us, event | category | flops | bytes accessed | tf_op | source)
XLA Modules:
  0.0 56.9 jit_solution(6587750853658595528)
XLA Ops:
  0.0 56.2 %shard_map.118 = bf16[128,1024]{1,0:T(8,128)(2,1)S(1)} custom-call(bf16[128,1024]{1,0:T(8,128)(2,1)} %q_hbm.1, bf16[128,1024]{1,0:T(8,128)(2,1)} %k_hbm.1, bf16[128,1024]{1,0:T(8,128)(2,1)} %v_hbm.1, f32[3,3,1024]{2,1,0:T(4,128)} %taps_hbm.1, f32[1,1024]{1,0:T(1,128)} %bitcast.4, f32[1,1024]{1,0:T(1,128)} %bitcast.5, f32[4,128,1024]{2,1,0:T(8,128)} %bitcast.3, ...), custom_call_target="tpu_custom_call" | custom-call | tf_op jit(solution)/shard_map/pallas_call | solution.py:416
  56.2 0.7 %copy.14 = bf16[128,1024]{1,0:T(8,128)(2,1)} copy(bf16[128,1024]{1,0:T(8,128)(2,1)S(1)} %shard_map.118) | data formatting | bytes 524288

commit v5 on v4

--- a/solution.py
+++ b/solution.py
@@ -235,17 +235,16 @@
 
     lax.fori_loop(0, tiles, mix, 0)
 
-    def send_mixed(i, _):
+    def send_bound(i, _):
         to = lax.rem(me + i, n)
-        for src, dst, sems in ((scale_send, scale_recv, scale_sems), (x_send.at[to], x_recv, x_sems)):
-            pltpu.make_async_remote_copy(
-                src_ref=src, dst_ref=dst.at[me], send_sem=sems.at[0], recv_sem=sems.at[1],
-                device_id=(to, column), device_id_type=MESH,
-            ).start()
+        pltpu.make_async_remote_copy(
+            src_ref=scale_send, dst_ref=scale_recv.at[me], send_sem=scale_sems.at[0], recv_sem=scale_sems.at[1],
+            device_id=(to, column), device_id_type=MESH,
+        ).start()
         return 0
 
-    lax.fori_loop(1, n, send_mixed, 0)
-    x_recv[pl.ds(me, 1)] = x_send[pl.ds(me, 1)]
+    exchange(x_send, x_recv, x_sems)
+    lax.fori_loop(1, n, send_bound, 0)
     scale_recv[pl.ds(me, 1)] = scale_send[...].reshape(1, 1, 128)
     send_filter(1)
     for h in range(2, PARTS):

time: 57 us -> 57.5 us (level)
  no operation moved by 1% of the time
where the time goes in v5:
time: 57.5 us; the launch traced here: 57.4 us
  Pallas kernels  56.7 us (99%)
  local copies, waits for them, and re-layouts  0.71 us (1%)
    pallas_call x1, Pallas kernels, per_device(): pl.pallas_call(functools.partial(kernel, n, n_ch, float(width * n_ch)), o...  56.7 us

profile of v5, /device:TPU:1, one launch (start us, length us, event | category | flops | bytes accessed | tf_op | source)
XLA Modules:
  0.0 57.4 jit_solution(2596471442623560804)
XLA Ops:
  0.0 56.7 %shard_map.118 = bf16[128,1024]{1,0:T(8,128)(2,1)S(1)} custom-call(bf16[128,1024]{1,0:T(8,128)(2,1)} %q_hbm.1, bf16[128,1024]{1,0:T(8,128)(2,1)} %k_hbm.1, bf16[128,1024]{1,0:T(8,128)(2,1)} %v_hbm.1, f32[3,3,1024]{2,1,0:T(4,128)} %taps_hbm.1, f32[1,1024]{1,0:T(1,128)} %bitcast.4, f32[1,1024]{1,0:T(1,128)} %bitcast.5, f32[4,128,1024]{2,1,0:T(8,128)} %bitcast.3, ...), custom_call_target="tpu_custom_call" | custom-call | tf_op jit(solution)/shard_map/pallas_call | solution.py:415
  56.7 0.7 %copy.14 = bf16[128,1024]{1,0:T(8,128)(2,1)} copy(bf16[128,1024]{1,0:T(8,128)(2,1)S(1)} %shard_map.118) | data formatting | bytes 524288

commit v6 on v4

--- a/solution.py
+++ b/solution.py
@@ -16,7 +16,7 @@
 LN2 = float(np.log(2.0))
 IN_MAX = 6.0
 PARTS = 4
-GROUPS = 4
+GROUPS = 2
 
 
 class Code:

time: 57 us -> 57 us (level)
  no operation moved by 1% of the time
where the time goes in v6:
time: 57 us; the launch traced here: 56.9 us
  Pallas kernels  56.2 us (99%)
  local copies, waits for them, and re-layouts  0.71 us (1%)
    pallas_call x1, Pallas kernels, per_device(): pl.pallas_call(functools.partial(kernel, n, n_ch, float(width * n_ch)), o...  56.2 us

profile of v6, /device:TPU:1, one launch (start us, length us, event | category | flops | bytes accessed | tf_op | source)
XLA Modules:
  0.0 56.9 jit_solution(5000201452905626118)
XLA Ops:
  0.0 56.2 %shard_map.118 = bf16[128,1024]{1,0:T(8,128)(2,1)S(1)} custom-call(bf16[128,1024]{1,0:T(8,128)(2,1)} %q_hbm.1, bf16[128,1024]{1,0:T(8,128)(2,1)} %k_hbm.1, bf16[128,1024]{1,0:T(8,128)(2,1)} %v_hbm.1, f32[3,3,1024]{2,1,0:T(4,128)} %taps_hbm.1, f32[1,1024]{1,0:T(1,128)} %bitcast.4, f32[1,1024]{1,0:T(1,128)} %bitcast.5, f32[4,128,1024]{2,1,0:T(8,128)} %bitcast.3, ...), custom_call_target="tpu_custom_call" | custom-call | tf_op jit(solution)/shard_map/pallas_call | solution.py:416
  56.2 0.7 %copy.14 = bf16[128,1024]{1,0:T(8,128)(2,1)} copy(bf16[128,1024]{1,0:T(8,128)(2,1)S(1)} %shard_map.118) | data formatting | bytes 524288
